TPU v7x, 128 devices: a whole 4x4x4 slice. The times are simulated.
128 devices in a mesh: node: 8 (over x_hi, z), local: 16 (over y, x_lo, core).
Axes of the slice: x: 4 (x_hi: 2, x_lo: 2; x = x_hi * 2 + x_lo), y: 4, z: 4, core: 2. Of those that a mesh axis runs over, the one named last changes fastest.
Arguments:
- hidden_acts: bfloat16 [163840, 1024], P(('node', 'local')), may hold values from -8 to 8
- grad_out: bfloat16 [163840, 8192], P(('node', 'local')), may hold values from -0.0390625 to 0.0390625
Outputs:
- grad_shard: float32 [1024, 8192], P(('node', 'local'))
All inputs are finite; a program needn't handle non-finite values.
Results may differ from a plain program's by a relative error of at most 0.0003.
Values may be sent and summed in bfloat16 or wider, within the bound.
A program may use at most 256 MiB of HBM per device.

v0:
```python
import jax
import jax.numpy as jnp
from jax import lax
from jax.sharding import PartitionSpec as P

QB = 128


def unit_of(block_peak):
    power_two = jnp.full_like(block_peak, 2.0 ** (-64))
    for exponent in (64, 32, 16, 8, 4, 2, 1):
        candidate = power_two * 2.0**exponent
        power_two = jnp.where(candidate <= block_peak, candidate, power_two)
    return power_two / 64.0


def quantize(values):
    blocked = values.reshape(values.shape[:-1] + (values.shape[-1] // QB, QB))
    block_peak = jnp.max(jnp.abs(blocked), axis=-1, keepdims=True)
    block_unit = unit_of(block_peak)
    levels = jnp.clip(jnp.floor(blocked / block_unit + 0.5), -127.0, 127.0)
    return (levels * block_unit).astype(jnp.bfloat16).reshape(values.shape)


def settle_node(pieces):
    return quantize(jnp.sum(pieces, axis=1, dtype=jnp.float32))


def per_device(hidden_acts, grad_out):
    count_local = lax.axis_size("local")
    count_node = lax.axis_size("node")
    row_count = hidden_acts.shape[1]
    feature_width = grad_out.shape[1]
    block_rows = row_count // (count_node * count_local)
    partial_value = lax.dot_general(
        hidden_acts, grad_out, (((0,), (0,)), ((), ())), preferred_element_type=jnp.float32
    )
    quantized = quantize(partial_value).reshape(count_node, count_local, block_rows, feature_width)
    node_quant = settle_node(
        lax.all_to_all(quantized, "local", split_axis=1, concat_axis=1, tiled=True)
    )
    arrived = lax.all_to_all(node_quant, "node", split_axis=0, concat_axis=0, tiled=True)
    return jnp.sum(arrived, axis=0, dtype=jnp.float32)


def solution(mesh):
    return jax.shard_map(
        per_device,
        mesh=mesh,
        in_specs=(P(("node", "local"), None), P(("node", "local"), None)),
        out_specs=P(("node", "local"), None),
        check_vma=False,
    )
```

profile of v0, /device:TPU:0, one launch (start us, length us, event | category | flops | bytes accessed | tf_op | source)
XLA Modules:
  0.0 383.5 jit_solution(5173093611001492906)
XLA Ops:
  0.0 0.0 copy-start
  0.0 1.7 copy-done
  1.7 28.4 %fusion.6 = f32[1024,8192]{1,0:T(8,128)} fusion(bf16[1280,1024]{1,0:T(8,128)(2,1)S(1)} %copy-done, bf16[1280,8192]{1,0:T(8,128)(2,1)} %param.3), kind=kOutput, calls=%fused_computation.25 | convolution fusion | flops 21474836480 | bytes 57147392 | tf_op jit(solution)/shard_map/dot_general | solution.py:35
  30.1 12.3 %abs_bitcast_fusion = f32[128,8,64,128]{3,1,2,0:T(8,128)S(1)} fusion(f32[1024,8192]{1,0:T(8,128)} %fusion.6), kind=kLoop, calls=%fused_computation.2 | loop fusion | flops 8388608 | bytes 67108864
  42.4 12.2 %copy.6 = f32[128,8,64,128]{3,2,1,0:T(8,128)} copy(f32[128,8,64,128]{3,1,2,0:T(8,128)S(1)} %abs_bitcast_fusion) | data formatting | bytes 67108864
  54.6 15.3 %reduce_max.18 = f32[1024,64]{1,0:T(8,128)S(1)} reduce(f32[1024,64,128]{2,1,0:T(8,128)} %bitcast.22, f32[]{:T(128)} %constant.16.clone.1), dimensions={2}, to_apply=%region_0.0 | reduce | flops 8323072 | bytes 33816580 | tf_op jit(solution)/shard_map/reduce_max | solution.py:19
  69.9 0.4 fusion.4
  70.3 21.5 %div.36 = f32[1024,64,128]{2,1,0:T(8,128)} broadcast(f32[1024,64]{1,0:T(8,128)S(1)} %fusion.4), dimensions={0,1} | broadcast | bytes 33816576 | tf_op jit(solution)/shard_map/div | solution.py:21
  91.7 35.9 %div.37 = f32[8,16,8,8192]{3,2,1,0:T(8,128)} reshape(f32[1024,64,128]{2,1,0:T(8,128)} %div.36) | data formatting | bytes 67108864 | tf_op jit(solution)/shard_map/div | solution.py:21
  127.6 27.8 %multiply_convert_fusion = bf16[8,16,8,8192]{3,2,1,0:T(8,128)(2,1)} fusion(f32[8,16,8,8192]{3,2,1,0:T(8,128)} %div.37, f32[8,16,8,8192]{3,2,1,0:T(8,128)} %bitcast.21), kind=kLoop, calls=%fused_computation.1 | loop fusion | flops 50331648 | bytes 83886080 | tf_op jit(solution)/shard_map/convert_element_type | solution.py:22
  155.3 8.6 %copy.5 = bf16[8,16,8,8192]{3,2,0,1:T(8,128)(2,1)S(1)} copy(bf16[8,16,8,8192]{3,2,1,0:T(8,128)(2,1)} %multiply_convert_fusion) | data formatting | bytes 33554432 | tf_op jit(solution)/shard_map/convert_element_type | solution.py:22
  163.9 0.0 copy-start.1
  163.9 190.7 %all_to_all.10 = bf16[8,16,8,8192]{3,2,0,1:T(8,128)(2,1)S(1)} all-to-all(bf16[8,16,8,8192]{3,2,0,1:T(8,128)(2,1)S(1)} %copy.5), channel_id=1, replica_groups=mesh['node'=8,'local'=16] {'local'}, dimensions={1} | all-to-all | bytes 33554432 | tf_op jit(solution)/shard_map/all_to_all | solution.py:40
  354.6 2.6 convert_reduce_fusion
  357.2 0.6 bitcast_reduce_fusion
  357.8 0.2 fusion.5
  358.0 0.8 fusion.3
  358.7 23.9 %all_to_all.11 = bf16[8,8,8192]{2,1,0:T(8,128)(2,1)S(1)} all-to-all(bf16[8,8,8192]{2,1,0:T(8,128)(2,1)S(1)} %fusion.3), channel_id=1, replica_groups=mesh['node'=8,'local'=16] {'node'}, dimensions={0} | all-to-all | bytes 2097152 | tf_op jit(solution)/shard_map/all_to_all | solution.py:42
  382.7 0.8 convert_reduce_fusion.1
  383.5 0.0 copy-done.1
Async XLA Ops:
  0.0 1.7 copy-start
  163.9 219.6 %copy-start.1 = (bf16[1280,1024]{1,0:T(8,128)(2,1)S(1)}, bf16[1280,1024]{1,0:T(8,128)(2,1)}, u32[]{:S(2)}) copy-start(bf16[1280,1024]{1,0:T(8,128)(2,1)} %param.2) | copy-start | bytes 7864324
where the time goes:
time: 385 us; the launch traced here: 384 us
  blocking collectives  215 us (56%)
  local copies, waits for them, and re-layouts  79.8 us (21%)
  other arithmetic  60.7 us (16%)
  matrix products  28.4 us (7%)
    all_to_all x1, blocking collectives, per_device(): lax.all_to_all(quantized, 'local', split_axis=1, concat_axis=1, tiled=True)  191 us
    div x2, local copies, waits for them, and re-layouts, quantize(): levels = jnp.clip(jnp.floor(blocked / block_unit + 0.5), -127.0, 127.0)  57.3 us
    convert_element_type x2, other arithmetic, quantize(): return (levels * block_unit).astype(jnp.bfloat16).reshape(values.shape)  28.5 us
    dot_general x1, matrix products, per_device(): lax.dot_general(hidden_acts, grad_out, (((0,), (0,)), ((), ())), preferre...  28.4 us
    all_to_all x1, blocking collectives, per_device(): lax.all_to_all(node_quant, 'node', split_axis=0, concat_axis=0, tiled=True)  23.9 us
    reduce_max x2, other arithmetic, quantize(): block_peak = jnp.max(jnp.abs(blocked), axis=-1, keepdims=True)  15.9 us
    unnamed x5, local copies, waits for them, and re-layouts  13.9 us
    unnamed x1, other arithmetic  12.3 us

commit v1 on v0

v1 whole, which is shorter than its diff:
```python
import functools

import jax
import jax.numpy as jnp
from jax import lax
from jax.experimental import pallas as pl
from jax.experimental.pallas import tpu as pltpu
from jax.sharding import PartitionSpec as P

QB = 128
NY, NX, NC = 4, 2, 2
N_NODE = 8
NODE_A = 3
NODE_B = N_NODE - NODE_A
ROWS_A, ROWS_B = 8 * NODE_A, 8 * NODE_B
SEC_A, SEC_B = NX * NY * ROWS_A, NX * NY * ROWS_B
HALF = SEC_A + SEC_B
COLS = 256
SLOTS = 8
LAG = (1, 3, 5, 7, 9)
MESH = pl.DeviceIdType.MESH
F32, BF16 = jnp.float32, jnp.bfloat16


def quantize(values):
    peak = jnp.max(jnp.abs(values), axis=-1, keepdims=True)
    scaled = peak * (2.0**23 + 1.0)
    power = scaled - scaled * (1.0 - 2.0**-24)
    power = jnp.minimum(jnp.maximum(power, 2.0**-64), 2.0**63)
    levels = jnp.floor(values * (64.0 / power) + 0.5)
    return jnp.minimum(jnp.maximum(levels, -127.0), 127.0) * (power * (1.0 / 64.0))


def kernel(
    chunks, ht, grad, out,
    gbuf, qsend, qrecv, sa, sb, xa, y1a, y2a, y1b, y2b, xb, ns, nr,
    gsem, core_s, core_r, x_s, x_r, y1_s, y1_r, y2_s, y2_r, node_s, node_r,
):
    me = lax.axis_index("node")
    loc = lax.axis_index("local")
    c, x, y = loc % NC, (loc // NC) % NX, loc // (NC * NX)
    up, down, far = (y + 1) % NY, (y + NY - 1) % NY, (y + 2) % NY
    sibling = {"local": loc + 1 - 2 * c}
    across = {"local": loc + NC * (1 - 2 * x)}
    above = {"local": (up * NX + x) * NC + c}
    below = {"local": (down * NX + x) * NC + c}
    other = 1 - x
    half = COLS // 2

    def remote(src, dst, s, r, device):
        return pltpu.make_async_remote_copy(
            src_ref=src, dst_ref=dst, send_sem=s, recv_sem=r, device_id=device, device_id_type=MESH
        )

    def load(t):
        cols = pl.ds(pl.multiple_of(t * COLS, COLS), COLS)
        return pltpu.make_async_copy(grad.at[:, cols], gbuf.at[t % 3], gsem.at[t % 3])

    def core_copy(t):
        return remote(qsend.at[t % 4], qrecv.at[t], core_s.at[t % SLOTS], core_r.at[t % SLOTS], sibling)

    def x_copies(t):
        k = t % SLOTS
        return (
            remote(sa.at[t, other], xa.at[t], x_s.at[k, 0], x_r.at[k, 0], across),
            remote(sb.at[t, y, other], xb.at[t], x_s.at[k, 1], x_r.at[k, 1], across),
        )

    def y1_copies(t):
        k = t % SLOTS
        made = []
        for i, (src, dst) in enumerate(((sa.at[t, x, far], y1a), (sb.at[t, far], y1b))):
            for d, device in enumerate((above, below)):
                made.append(
                    remote(
                        src.at[..., pl.ds(d * half, half)], dst.at[t, d],
                        y1_s.at[k, i, d], y1_r.at[k, i, d], device,
                    )
                )
        return made[:2], made[2:]

    def y2_copies(t):
        k = t % SLOTS
        made = []
        for i in range(2):
            for d, (row, device) in enumerate(((up, above), (down, below))):
                src = (sa.at[t, x, row], sb.at[t, row])[i]
                made.append(
                    remote(src, (y2a, y2b)[i].at[t, d], y2_s.at[k, i, d], y2_r.at[k, i, d], device)
                )
        return made[:2], made[2:]

    def node_send(t, k):
        to = (me + k) % N_NODE
        return remote(
            ns.at[t, to], nr.at[t, me], node_s.at[t % SLOTS, k], node_r.at[t % SLOTS, k], {"node": to}
        )

    def node_recv(t, k):
        source = (me + N_NODE - k) % N_NODE
        return remote(
            ns.at[t, source], nr.at[t, source],
            node_s.at[t % SLOTS, k], node_r.at[t % SLOTS, k], {"node": source},
        )

    def start(copies):
        for copy in copies:
            copy.start()

    def wait(copies):
        for copy in copies:
            copy.wait()

    barrier = pltpu.get_barrier_semaphore()
    peers = [sibling, across, above, below] + [{"node": (me + k) % N_NODE} for k in range(1, N_NODE)]
    load(0).start()
    load(1).start()
    for peer in peers:
        pl.semaphore_signal(barrier, inc=1, device_id=peer, device_id_type=MESH)
    pl.semaphore_wait(barrier, len(peers))

    def compute(t):
        @pl.when(t + 2 < chunks)
        def _():
            load(t + 2).start()

        load(t).wait()

        @pl.when(t >= 4)
        def _():
            core_copy(t - 4).wait_send()

        block = gbuf.at[t % 3]
        for first, count in ((0, 256), (256, 256)):
            rows = pl.ds(pl.multiple_of((1 - c) * HALF + first, 64), count)
            part = jnp.dot(ht[rows, :], block[...], preferred_element_type=F32)
            for j in range(COLS // QB):
                cut = slice(j * QB, (j + 1) * QB)
                qsend[t % 4, first : first + count, cut] = quantize(part[:, cut]).astype(BF16)
        core_copy(t).start()
        for first, count, dst, shape in (
            (0, SEC_A, sa, (NX, NY, ROWS_A, QB)),
            (SEC_A, SEC_B, sb, (NY, NX, ROWS_B, QB)),
        ):
            rows = pl.ds(pl.multiple_of(c * HALF + first, 64), count)
            part = jnp.dot(ht[rows, :], block[...], preferred_element_type=F32)
            for j in range(COLS // QB):
                cut = slice(j * QB, (j + 1) * QB)
                dst[t, :, :, :, cut] = quantize(part[:, cut]).reshape(shape)

    def stage1(t):
        core_copy(t).wait_recv()
        sa[t] = sa[t] + qrecv[t, :SEC_A].astype(F32).reshape(NX, NY, ROWS_A, COLS)
        x_copies(t)[0].start()
        sb[t] = sb[t] + qrecv[t, SEC_A:].astype(F32).reshape(NY, NX, ROWS_B, COLS)
        start(y1_copies(t)[1])

    def stage2(t):
        x_copies(t)[0].wait()
        sa[t, x] = sa[t, x] + xa[t]
        start(y1_copies(t)[0])
        wait(y1_copies(t)[1])
        sb[t, up, :, :, :half] = sb[t, up, :, :, :half] + y1b[t, 0]
        sb[t, down, :, :, half:] = sb[t, down, :, :, half:] + y1b[t, 1]
        start(y2_copies(t)[1])

    def stage3(t):
        wait(y1_copies(t)[0])
        sa[t, x, up, :, :half] = sa[t, x, up, :, :half] + y1a[t, 0]
        sa[t, x, down, :, half:] = sa[t, x, down, :, half:] + y1a[t, 1]
        start(y2_copies(t)[0])
        wait(y2_copies(t)[1])
        sb[t, y] = sb[t, y] + y2b[t, 0] + y2b[t, 1]
        x_copies(t)[1].start()

    def stage4(t):
        wait(y2_copies(t)[0])
        sum_a = sa[t, x, y] + y2a[t, 0] + y2a[t, 1]
        x_copies(t)[1].wait()
        sum_b = sb[t, y, x] + xb[t]
        for total, node, count in ((sum_a, 0, NODE_A), (sum_b, NODE_A, NODE_B)):
            pieces = [
                quantize(total[:, j * QB : (j + 1) * QB]).reshape(count, 8, QB) for j in range(COLS // QB)
            ]
            ns[t, node : node + count] = jnp.concatenate(pieces, axis=1).astype(BF16)
        for k in range(1, N_NODE):
            node_send(t, k).start()

    def stage5(t):
        total = ns[t, me].astype(F32)
        for k in range(1, N_NODE):
            node_send(t, k).wait_send()
            node_recv(t, k).wait_recv()
            total = total + nr[t, (me + N_NODE - k) % N_NODE].astype(F32)
        for j in range(COLS // QB):
            cols = pl.ds(pl.multiple_of(t * COLS + j * QB, QB), QB)
            out[:, cols] = total[8 * j : 8 * j + 8]

    def step(t, carry):
        pl.when(t < chunks)(lambda: compute(t))
        for lag, stage in zip(LAG, (stage1, stage2, stage3, stage4, stage5)):
            pl.when((t >= lag) & (t < chunks + lag))(functools.partial(stage, t - lag))
        return carry

    lax.fori_loop(0, chunks + LAG[-1], step, 0)
    for t in range(chunks - 4, chunks):
        core_copy(t).wait_send()


def per_device(hidden_acts, grad_out):
    tokens, width = grad_out.shape
    chunks = width // COLS
    blocked = hidden_acts.T.reshape(N_NODE, NY, NX, NC, 8, tokens)
    first = blocked[:NODE_A].transpose(3, 2, 1, 0, 4, 5).reshape(NC, SEC_A, tokens)
    second = blocked[NODE_A:].transpose(3, 1, 2, 0, 4, 5).reshape(NC, SEC_B, tokens)
    ht = jnp.concatenate([first, second], axis=1).reshape(NC * HALF, tokens)
    half = COLS // 2
    vmem, dma = pltpu.VMEM, pltpu.SemaphoreType.DMA
    return pl.pallas_call(
        functools.partial(kernel, chunks),
        out_shape=jax.ShapeDtypeStruct((8, width), F32),
        in_specs=[pl.BlockSpec(memory_space=pltpu.VMEM), pl.BlockSpec(memory_space=pl.ANY)],
        out_specs=pl.BlockSpec(memory_space=pltpu.VMEM),
        scratch_shapes=[
            vmem((3, tokens, COLS), BF16),
            vmem((4, HALF, COLS), BF16),
            vmem((chunks, HALF, COLS), BF16),
            vmem((chunks, NX, NY, ROWS_A, COLS), F32),
            vmem((chunks, NY, NX, ROWS_B, COLS), F32),
            vmem((chunks, NY, ROWS_A, COLS), F32),
            vmem((chunks, 2, ROWS_A, half), F32),
            vmem((chunks, 2, ROWS_A, COLS), F32),
            vmem((chunks, 2, NX, ROWS_B, half), F32),
            vmem((chunks, 2, NX, ROWS_B, COLS), F32),
            vmem((chunks, ROWS_B, COLS), F32),
            vmem((chunks, N_NODE, 16, half), BF16),
            vmem((chunks, N_NODE, 16, half), BF16),
            dma((3,)),
            dma((SLOTS,)),
            dma((SLOTS,)),
            dma((SLOTS, 2)),
            dma((SLOTS, 2)),
            dma((SLOTS, 2, 2)),
            dma((SLOTS, 2, 2)),
            dma((SLOTS, 2, 2)),
            dma((SLOTS, 2, 2)),
            dma((SLOTS, N_NODE)),
            dma((SLOTS, N_NODE)),
        ],
        compiler_params=pltpu.CompilerParams(
            collective_id=0, has_side_effects=True, vmem_limit_bytes=58 * 2**20
        ),
        cost_estimate=pl.CostEstimate(
            flops=2 * tokens * NC * HALF * width, bytes_accessed=2 * tokens * (width + NC * HALF), transcendentals=0
        ),
    )(ht, grad_out)


def solution(mesh):
    return jax.shard_map(
        per_device,
        mesh=mesh,
        in_specs=(P(("node", "local"), None), P(("node", "local"), None)),
        out_specs=P(("node", "local"), None),
        check_vma=False,
    )
```

time: 385 us -> 143 us (0.37)
  blocking collectives: 215 us -> 0 us
  Pallas kernels: 0 us -> 136 us
  local copies, waits for them, and re-layouts: 79.8 us -> 4.99 us
  other arithmetic: 60.7 us -> 1.67 us
  matrix products: 28.4 us -> 0 us
    all_to_all x2 -> x0, blocking collectives: 215 us -> none  [the longest x1 191 us: per_device(): lax.all_to_all(quantized, 'local', split_axis=1, concat_axis=1, tiled=True)]
    pallas_call x0 -> x1, Pallas kernels: none -> 136 us  [per_device(): pl.pallas_call(functools.partial(kernel, chunks), out_shape=jax.ShapeDtyp...]
    div x2 -> x0, local copies, waits for them, and re-layouts: 57.3 us -> none  [quantize(): levels = jnp.clip(jnp.floor(blocked / block_unit + 0.5), -127.0, 127.0)]
    convert_element_type x2 -> x0, other arithmetic: 28.5 us -> none  [quantize(): return (levels * block_unit).astype(jnp.bfloat16).reshape(values.shape)]
    dot_general x1 -> x0, matrix products: 28.4 us -> none  [per_device(): lax.dot_general(hidden_acts, grad_out, (((0,), (0,)), ((), ())), preferre...]
    reduce_max x2 -> x0, other arithmetic: 15.9 us -> none  [quantize(): block_peak = jnp.max(jnp.abs(blocked), axis=-1, keepdims=True)]
    unnamed x1 -> x0, other arithmetic: 12.3 us -> none
    unnamed x5 -> x2, local copies, waits for them, and re-layouts: 13.9 us -> 4.65 us
where the time goes in v1:
time: 143 us
  Pallas kernels  136 us (95%)
  local copies, waits for them, and re-layouts  4.99 us (3%)
  other arithmetic  1.67 us (1%)
    pallas_call x1, Pallas kernels, per_device(): pl.pallas_call(functools.partial(kernel, chunks), out_shape=jax.ShapeDtyp...  136 us
    unnamed x2, local copies, waits for them, and re-layouts  4.65 us

profile of v1, /device:TPU:0, one launch (start us, length us, event | category | flops | bytes accessed | tf_op | source)
XLA Modules:
  0.0 143.1 jit_solution(5889206307334482501)
XLA Ops:
  0.0 3.0 %copy.6 = bf16[1280,1024]{0,1:T(8,128)(2,1)S(1)} copy(bf16[1280,1024]{1,0:T(8,128)(2,1)} %param.2) | data formatting | bytes 5242880 | tf_op args[0]
  3.0 0.1 slice.16
  3.1 0.1 slice.17
  3.2 0.1 copy.8
  3.3 0.1 copy.7
  3.4 1.7 %pad_maximum_fusion = bf16[2,512,1280]{2,1,0:T(8,128)(2,1)} fusion(bf16[2,320,1280]{2,1,0:T(8,128)(2,1)S(1)} %bitcast.12, bf16[2,192,1280]{2,1,0:T(8,128)(2,1)S(1)} %bitcast.14), kind=kLoop, calls=%fused_computation | loop fusion | flops 5242880 | bytes 5242880 | tf_op jit(solution)/shard_map/concatenate | solution.py:216
  5.0 136.4 %shard_map.28 = f32[8,8192]{1,0:T(8,128)} custom-call(bf16[1024,1280]{1,0:T(8,128)(2,1)} %bitcast.16, bf16[1280,8192]{1,0:T(8,128)(2,1)} %grad.1), custom_call_target="tpu_custom_call" | custom-call | flops 21474836480 | bytes 23592960 | tf_op jit(solution)/shard_map/pallas_call | solution.py:219
  141.4 1.7 %copy.10 = f32[8,8192]{1,0:T(8,128)} copy(f32[8,8192]{1,0:T(8,128)} %shard_map.28) | data formatting | bytes 524288

commit v2 on v1

--- a/solution.py
+++ b/solution.py
@@ -28,10 +28,12 @@
     power = scaled - scaled * (1.0 - 2.0**-24)
     power = jnp.minimum(jnp.maximum(power, 2.0**-64), 2.0**63)
     levels = jnp.floor(values * (64.0 / power) + 0.5)
-    return jnp.minimum(jnp.maximum(levels, -127.0), 127.0) * (power * (1.0 / 64.0))
-
-
-def kernel(
+    unit = power * (1.0 / 64.0)
+    levels = jnp.minimum(jnp.maximum(levels, -127.0), 127.0)
+    return levels * unit, jnp.where(peak > 0.0, unit, 2.0**57)
+
+
+def wide_kernel(
     chunks, ht, grad, out,
     gbuf, qsend, qrecv, sa, sb, xa, y1a, y2a, y1b, y2b, xb, ns, nr,
     gsem, core_s, core_r, x_s, x_r, y1_s, y1_r, y2_s, y2_r, node_s, node_r,
@@ -136,7 +138,7 @@
             part = jnp.dot(ht[rows, :], block[...], preferred_element_type=F32)
             for j in range(COLS // QB):
                 cut = slice(j * QB, (j + 1) * QB)
-                qsend[t % 4, first : first + count, cut] = quantize(part[:, cut]).astype(BF16)
+                qsend[t % 4, first : first + count, cut] = quantize(part[:, cut])[0].astype(BF16)
         core_copy(t).start()
         for first, count, dst, shape in (
             (0, SEC_A, sa, (NX, NY, ROWS_A, QB)),
@@ -146,7 +148,7 @@
             part = jnp.dot(ht[rows, :], block[...], preferred_element_type=F32)
             for j in range(COLS // QB):
                 cut = slice(j * QB, (j + 1) * QB)
-                dst[t, :, :, :, cut] = quantize(part[:, cut]).reshape(shape)
+                dst[t, :, :, :, cut] = quantize(part[:, cut])[0].reshape(shape)
 
     def stage1(t):
         core_copy(t).wait_recv()
@@ -180,7 +182,7 @@
         sum_b = sb[t, y, x] + xb[t]
         for total, node, count in ((sum_a, 0, NODE_A), (sum_b, NODE_A, NODE_B)):
             pieces = [
-                quantize(total[:, j * QB : (j + 1) * QB]).reshape(count, 8, QB) for j in range(COLS // QB)
+                quantize(total[:, j * QB : (j + 1) * QB])[0].reshape(count, 8, QB) for j in range(COLS // QB)
             ]
             ns[t, node : node + count] = jnp.concatenate(pieces, axis=1).astype(BF16)
         for k in range(1, N_NODE):
@@ -207,53 +209,356 @@
         core_copy(t).wait_send()
 
 
-def per_device(hidden_acts, grad_out):
-    tokens, width = grad_out.shape
-    chunks = width // COLS
+def split_power(words):
+    scaled = words * (2.0**23 + 1.0)
+    return scaled - scaled * (1.0 - 2.0**-24)
+
+
+def unpack(words):
+    signed = split_power(words)
+    both = words - signed
+    scale = jnp.abs(signed)
+    magic = scale * 6144.0
+    first = (both + magic) - magic
+    return first, both - first, scale
+
+
+def packed_kernel(
+    chunks, ht, grad, out, flag_out,
+    gbuf, qsend, qrecv, own, sa, sb,
+    xas, y1as, y2as, y1bs, y2bs, xbs, xa, y1a, y2a, y1b, y2b, xb, ns, nr, flag, fsend, frecv,
+    gsem, core_s, core_r, x_s, x_r, y1_s, y1_r, y2_s, y2_r, node_s, node_r, flag_s, flag_r,
+):
+    me = lax.axis_index("node")
+    loc = lax.axis_index("local")
+    c, x, y = loc % NC, (loc // NC) % NX, loc // (NC * NX)
+    far = (y + 2) % NY
+    other = 1 - x
+
+    def at_y(row):
+        return {"local": (row * NX + x) * NC + c}
+
+    sibling = {"local": loc + 1 - 2 * c}
+    across = {"local": loc + NC * (1 - 2 * x)}
+    ring = [at_y((y + k) % NY) for k in (1, 3, 2)]
+
+    def remote(src, dst, s, r, device):
+        return pltpu.make_async_remote_copy(
+            src_ref=src, dst_ref=dst, send_sem=s, recv_sem=r, device_id=device, device_id_type=MESH
+        )
+
+    def load(t):
+        cols = pl.ds(pl.multiple_of(t * COLS, COLS), COLS)
+        return pltpu.make_async_copy(grad.at[:, cols], gbuf.at[t % 3], gsem.at[t % 3])
+
+    def core_copy(t):
+        return remote(qsend.at[t % 4], qrecv.at[t], core_s.at[t % SLOTS], core_r.at[t % SLOTS], sibling)
+
+    def turn(t, part):
+        odd = (t + part) % 2
+        return (y + 1 + 2 * odd) % NY, (y + 3 - 2 * odd) % NY
+
+    def xa_copy(t):
+        k = t % SLOTS
+        return remote(xas.at[k], xa.at[t], x_s.at[k, 0], x_r.at[k, 0], across)
+
+    def xb_copy(t):
+        k = t % SLOTS
+        return remote(xbs.at[k], xb.at[t], x_s.at[k, 1], x_r.at[k, 1], across)
+
+    def y1_copy(t, part):
+        k = t % SLOTS
+        src, dst = ((y1as, y1a), (y1bs, y1b))[part]
+        return remote(src.at[k], dst.at[t], y1_s.at[k, part], y1_r.at[k, part], at_y(turn(t, part)[0]))
+
+    def y2_copy(t, part, late):
+        k = t % SLOTS
+        src, dst = ((y2as, y2a), (y2bs, y2b))[part]
+        return remote(
+            src.at[k, late], dst.at[t, late], y2_s.at[k, part, late], y2_r.at[k, part, late],
+            at_y(turn(t, part)[1 - late]),
+        )
+
+    def node_send(t, k):
+        to = (me + k) % N_NODE
+        return remote(
+            ns.at[t % SLOTS, to], nr.at[t, me], node_s.at[t % SLOTS, k], node_r.at[t % SLOTS, k], {"node": to}
+        )
+
+    def node_recv(t, k):
+        source = (me + N_NODE - k) % N_NODE
+        return remote(
+            ns.at[t % SLOTS, source], nr.at[t, source],
+            node_s.at[t % SLOTS, k], node_r.at[t % SLOTS, k], {"node": source},
+        )
+
+    def pack(first, second, scale):
+        both = first + second
+        excess = jnp.maximum(jnp.abs(both), jnp.abs(second) * 4096.0) - scale
+        flag[...] = jnp.maximum(flag[...], jnp.max(excess.reshape(-1, 8, QB), axis=0))
+        return both + jnp.where(both < 0.0, -scale, scale)
+
+    def join(left, right):
+        return left[0] + right[0], left[1] + right[1], jnp.minimum(left[2], right[2])
+
+    def rows_of(index, count):
+        return pl.ds(pl.multiple_of(index * count, 8), count)
+
+    barrier = pltpu.get_barrier_semaphore()
+    peers = [sibling, across] + ring + [{"node": (me + k) % N_NODE} for k in range(1, N_NODE)]
+    load(0).start()
+    load(1).start()
+    for peer in peers:
+        pl.semaphore_signal(barrier, inc=1, device_id=peer, device_id_type=MESH)
+    flag[...] = jnp.full((8, QB), -1.0, F32)
+    pl.semaphore_wait(barrier, len(peers))
+
+    def compute(t):
+        @pl.when(t + 2 < chunks)
+        def _():
+            load(t + 2).start()
+
+        load(t).wait()
+
+        @pl.when(t >= 4)
+        def _():
+            core_copy(t - 4).wait_send()
+
+        block = gbuf.at[t % 3]
+        for mine in (0, 1):
+            for first, count in ((0, 256), (256, 256)):
+                start = (c if mine else 1 - c) * HALF + first
+                rows = pl.ds(pl.multiple_of(start, 256), count)
+                part = jnp.dot(ht[rows, :], block[...], preferred_element_type=F32)
+                one, unit_one = quantize(part[:, :QB])
+                two, unit_two = quantize(part[:, QB:])
+                scale = jnp.minimum(unit_one, unit_two) * 2.0**23
+                one = one * 4096.0
+                if mine:
+                    own[t % 2, 0, first : first + count] = one
+                    own[t % 2, 1, first : first + count] = two
+                    own[t % 2, 2, first : first + count] = jnp.broadcast_to(scale, (count, QB))
+                else:
+                    qsend[t % 4, first : first + count] = pack(one, two, scale)
+            if not mine:
+                core_copy(t).start()
+
+    def stage1(t):
+        k = t % SLOTS
+        core_copy(t).wait_recv()
+
+        def pair(first, index, count):
+            rows = pl.ds(pl.multiple_of(first + index * count, 8), count)
+            return join(unpack(qrecv[t, rows]), tuple(own[t % 2, i, rows] for i in range(3)))
+
+        xas[k] = pack(*pair(0, other, NY * ROWS_A))
+        xa_copy(t).start()
+        ahead, behind = turn(t, 1)
+        y1bs[k] = pack(*pair(SEC_A, far, NX * ROWS_B))
+        y1_copy(t, 1).start()
+        y2bs[k, 0] = pack(*pair(SEC_A, behind, NX * ROWS_B))
+        y2_copy(t, 1, 0).start()
+        for i, value in enumerate(pair(0, x, NY * ROWS_A)):
+            sa[k, i] = value
+        for j, row in enumerate((ahead, y)):
+            for i, value in enumerate(pair(SEC_A, row, NX * ROWS_B)):
+                sb[k, j, i] = value
+
+    def stage2(t):
+        k = t % SLOTS
+        xa_copy(t).wait()
+
+        def pair(row):
+            rows = rows_of(row, ROWS_A)
+            return join(unpack(xa[t, rows]), tuple(sa[k, i, rows] for i in range(3)))
+
+        ahead, behind = turn(t, 0)
+        y1as[k] = pack(*pair(far))
+        y1_copy(t, 0).start()
+        y2as[k, 0] = pack(*pair(behind))
+        y2_copy(t, 0, 0).start()
+        for row in (ahead, y):
+            for i, value in enumerate(pair(row)):
+                sa[k, i, rows_of(row, ROWS_A)] = value
+        y1_copy(t, 1).wait()
+        y2bs[k, 1] = pack(*join(unpack(y1b[t]), tuple(sb[k, 0, i] for i in range(3))))
+        y2_copy(t, 1, 1).start()
+
+    def stage3(t):
+        k = t % SLOTS
+        y1_copy(t, 0).wait()
+        rows = rows_of(turn(t, 0)[0], ROWS_A)
+        y2as[k, 1] = pack(*join(unpack(y1a[t]), tuple(sa[k, i, rows] for i in range(3))))
+        y2_copy(t, 0, 1).start()
+        y2_copy(t, 1, 0).wait()
+        y2_copy(t, 1, 1).wait()
+
+        def pair(index):
+            rows = rows_of(index, ROWS_B)
+            held = tuple(sb[k, 1, i, rows] for i in range(3))
+            return join(join(unpack(y2b[t, 0, rows]), unpack(y2b[t, 1, rows])), held)
+
+        xbs[k] = pack(*pair(other))
+        xb_copy(t).start()
+        for i, value in enumerate(pair(x)[:2]):
+            sb[k, 0, i, :ROWS_B] = value
+
+    def stage4(t):
+        k = t % SLOTS
+        y2_copy(t, 0, 0).wait()
+        y2_copy(t, 0, 1).wait()
+        rows = rows_of(y, ROWS_A)
+        left, right = unpack(y2a[t, 0]), unpack(y2a[t, 1])
+        sum_a = [sa[k, i, rows] + left[i] + right[i] for i in range(2)]
+        xb_copy(t).wait()
+        last = unpack(xb[t])
+        sum_b = [sb[k, 0, i, :ROWS_B] + last[i] for i in range(2)]
+        for total, node, count in ((sum_a, 0, NODE_A), (sum_b, NODE_A, NODE_B)):
+            pieces = [
+                quantize(total[0] * (1.0 / 4096.0))[0].reshape(count, 8, QB),
+                quantize(total[1])[0].reshape(count, 8, QB),
+            ]
+            ns[k, node : node + count] = jnp.concatenate(pieces, axis=1).astype(BF16)
+        for j in range(1, N_NODE):
+            node_send(t, j).start()
+
+    def stage5(t):
+        total = ns[t % SLOTS, me].astype(F32)
+        for j in range(1, N_NODE):
+            node_send(t, j).wait_send()
+            node_recv(t, j).wait_recv()
+            total = total + nr[t, (me + N_NODE - j) % N_NODE].astype(F32)
+        for j in range(COLS // QB):
+            cols = pl.ds(pl.multiple_of(t * COLS + j * QB, QB), QB)
+            out[:, cols] = total[8 * j : 8 * j + 8]
+
+    rounds = ([sibling], [across], ring, [{"node": (me + k) % N_NODE} for k in range(1, N_NODE)])
+    places = (0, 1, 2, 5)
+
+    def flag_copies(index):
+        return [
+            remote(
+                fsend.at[index], frecv.at[places[index] + i],
+                flag_s.at[places[index] + i], flag_r.at[places[index] + i], device,
+            )
+            for i, device in enumerate(rounds[index])
+        ]
+
+    def flag_round(index):
+        value = flag[...] if index == 0 else fsend[index - 1]
+        if index:
+            for i, copy in enumerate(flag_copies(index - 1)):
+                copy.wait()
+                value = jnp.maximum(value, frecv[places[index - 1] + i])
+        if index == len(rounds):
+            flag_out[...] = value
+            return
+        fsend[index] = value
+        for copy in flag_copies(index):
+            copy.start()
+
+    def step(t, carry):
+        pl.when(t < chunks)(lambda: compute(t))
+        for lag, stage in zip(LAG, (stage1, stage2, stage3, stage4, stage5)):
+            pl.when((t >= lag) & (t < chunks + lag))(functools.partial(stage, t - lag))
+        for index in range(len(rounds)):
+            pl.when(t == chunks + LAG[2] + index)(functools.partial(flag_round, index))
+        return carry
+
+    lax.fori_loop(0, chunks + LAG[-1], step, 0)
+    flag_round(len(rounds))
+    for t in range(chunks - 4, chunks):
+        core_copy(t).wait_send()
+
+
+def arrange(hidden_acts):
+    tokens = hidden_acts.shape[0]
     blocked = hidden_acts.T.reshape(N_NODE, NY, NX, NC, 8, tokens)
     first = blocked[:NODE_A].transpose(3, 2, 1, 0, 4, 5).reshape(NC, SEC_A, tokens)
     second = blocked[NODE_A:].transpose(3, 1, 2, 0, 4, 5).reshape(NC, SEC_B, tokens)
-    ht = jnp.concatenate([first, second], axis=1).reshape(NC * HALF, tokens)
-    half = COLS // 2
-    vmem, dma = pltpu.VMEM, pltpu.SemaphoreType.DMA
+    return jnp.concatenate([first, second], axis=1).reshape(NC * HALF, tokens)
+
+
+def call(body, collective_id, ht, grad_out, extra_out, scratch):
+    tokens, width = grad_out.shape
+    vmem_spec = pl.BlockSpec(memory_space=pltpu.VMEM)
+    out_shape = [jax.ShapeDtypeStruct((8, width), F32)] + extra_out
     return pl.pallas_call(
-        functools.partial(kernel, chunks),
-        out_shape=jax.ShapeDtypeStruct((8, width), F32),
-        in_specs=[pl.BlockSpec(memory_space=pltpu.VMEM), pl.BlockSpec(memory_space=pl.ANY)],
-        out_specs=pl.BlockSpec(memory_space=pltpu.VMEM),
-        scratch_shapes=[
-            vmem((3, tokens, COLS), BF16),
-            vmem((4, HALF, COLS), BF16),
-            vmem((chunks, HALF, COLS), BF16),
-            vmem((chunks, NX, NY, ROWS_A, COLS), F32),
-            vmem((chunks, NY, NX, ROWS_B, COLS), F32),
-            vmem((chunks, NY, ROWS_A, COLS), F32),
-            vmem((chunks, 2, ROWS_A, half), F32),
-            vmem((chunks, 2, ROWS_A, COLS), F32),
-            vmem((chunks, 2, NX, ROWS_B, half), F32),
-            vmem((chunks, 2, NX, ROWS_B, COLS), F32),
-            vmem((chunks, ROWS_B, COLS), F32),
-            vmem((chunks, N_NODE, 16, half), BF16),
-            vmem((chunks, N_NODE, 16, half), BF16),
-            dma((3,)),
-            dma((SLOTS,)),
-            dma((SLOTS,)),
-            dma((SLOTS, 2)),
-            dma((SLOTS, 2)),
-            dma((SLOTS, 2, 2)),
-            dma((SLOTS, 2, 2)),
-            dma((SLOTS, 2, 2)),
-            dma((SLOTS, 2, 2)),
-            dma((SLOTS, N_NODE)),
-            dma((SLOTS, N_NODE)),
-        ],
+        functools.partial(body, width // COLS),
+        out_shape=out_shape,
+        in_specs=[vmem_spec, pl.BlockSpec(memory_space=pl.ANY)],
+        out_specs=[vmem_spec] * len(out_shape),
+        scratch_shapes=scratch,
         compiler_params=pltpu.CompilerParams(
-            collective_id=0, has_side_effects=True, vmem_limit_bytes=58 * 2**20
+            collective_id=collective_id, has_side_effects=True, vmem_limit_bytes=58 * 2**20
         ),
         cost_estimate=pl.CostEstimate(
             flops=2 * tokens * NC * HALF * width, bytes_accessed=2 * tokens * (width + NC * HALF), transcendentals=0
         ),
     )(ht, grad_out)
+
+
+def wide(ht, grad_out):
+    tokens, width = grad_out.shape
+    chunks, half = width // COLS, COLS // 2
+    vmem, dma = pltpu.VMEM, pltpu.SemaphoreType.DMA
+    scratch = [
+        vmem((3, tokens, COLS), BF16),
+        vmem((4, HALF, COLS), BF16),
+        vmem((chunks, HALF, COLS), BF16),
+        vmem((chunks, NX, NY, ROWS_A, COLS), F32),
+        vmem((chunks, NY, NX, ROWS_B, COLS), F32),
+        vmem((chunks, NY, ROWS_A, COLS), F32),
+        vmem((chunks, 2, ROWS_A, half), F32),
+        vmem((chunks, 2, ROWS_A, COLS), F32),
+        vmem((chunks, 2, NX, ROWS_B, half), F32),
+        vmem((chunks, 2, NX, ROWS_B, COLS), F32),
+        vmem((chunks, ROWS_B, COLS), F32),
+        vmem((chunks, N_NODE, 16, half), BF16),
+        vmem((chunks, N_NODE, 16, half), BF16),
+        dma((3,)),
+        *[dma((SLOTS,))] * 2,
+        *[dma((SLOTS, 2))] * 2,
+        *[dma((SLOTS, 2, 2))] * 4,
+        *[dma((SLOTS, N_NODE))] * 2,
+    ]
+    return call(wide_kernel, 1, ht, grad_out, [], scratch)[0]
+
+
+def packed(ht, grad_out):
+    tokens, width = grad_out.shape
+    chunks = width // COLS
+    vmem, dma = pltpu.VMEM, pltpu.SemaphoreType.DMA
+    sizes = [(NY * ROWS_A,), (ROWS_A,), (2, ROWS_A), (NX * ROWS_B,), (2, NX * ROWS_B), (ROWS_B,)]
+    scratch = [
+        vmem((3, tokens, COLS), BF16),
+        vmem((4, HALF, QB), F32),
+        vmem((chunks, HALF, QB), F32),
+        vmem((2, 3, HALF, QB), F32),
+        vmem((SLOTS, 3, NY * ROWS_A, QB), F32),
+        vmem((SLOTS, 2, 3, NX * ROWS_B, QB), F32),
+        *[vmem((SLOTS, *size, QB), F32) for size in sizes],
+        *[vmem((chunks, *size, QB), F32) for size in sizes],
+        vmem((SLOTS, N_NODE, 16, QB), BF16),
+        vmem((chunks, N_NODE, 16, QB), BF16),
+        vmem((8, QB), F32),
+        vmem((4, 8, QB), F32),
+        vmem((12, 8, QB), F32),
+        dma((3,)),
+        *[dma((SLOTS,))] * 2,
+        *[dma((SLOTS, 2))] * 4,
+        *[dma((SLOTS, 2, 2))] * 2,
+        *[dma((SLOTS, N_NODE))] * 2,
+        *[dma((12,))] * 2,
+    ]
+    out, flag = call(packed_kernel, 0, ht, grad_out, [jax.ShapeDtypeStruct((8, QB), F32)], scratch)
+    return out, jnp.max(flag) >= 0.0
+
+
+def per_device(hidden_acts, grad_out):
+    ht = arrange(hidden_acts)
+    out, misfit = packed(ht, grad_out)
+    return lax.cond(misfit, lambda: wide(ht, grad_out), lambda: out)
 
 
 def solution(mesh):

time: 143 us -> 122 us (0.85)
  Pallas kernels: 136 us -> 116 us
    pallas_call x1, Pallas kernels: 136 us -> 116 us  [call(): pl.pallas_call(functools.partial(body, width // COLS), out_shape=out_shap...]
    concatenate x1, other arithmetic: 1.67 us -> 0.17 us  [arrange(): return jnp.concatenate([first, second], axis=1).reshape(NC * HALF, tokens)]
where the time goes in v2:
time: 122 us
  Pallas kernels  116 us (95%)
  local copies, waits for them, and re-layouts  4.03 us (3%)
  other arithmetic  1.45 us (1%)
    pallas_call x1, Pallas kernels, call(): pl.pallas_call(functools.partial(body, width // COLS), out_shape=out_shap...  116 us
    unnamed x2, local copies, waits for them, and re-layouts  3.68 us

profile of v2, /device:TPU:0, one launch (start us, length us, event | category | flops | bytes accessed | tf_op | source)
XLA Modules:
  0.0 122.1 jit_solution(5248346012163795899)
XLA Ops:
  0.0 3.0 %copy.8 = bf16[1280,1024]{0,1:T(8,128)(2,1)S(1)} copy(bf16[1280,1024]{1,0:T(8,128)(2,1)} %param.4) | data formatting | bytes 5242880 | tf_op args[0]
  3.0 0.1 slice.16
  3.1 0.1 slice.17
  3.2 0.1 copy.10
  3.3 0.1 copy.9
  3.4 0.2 pad_maximum_fusion
  3.5 115.9 %shard_map.30 = (f32[8,8192]{1,0:T(8,128)S(1)}, f32[8,128]{1,0:T(8,128)}) custom-call(bf16[1024,1280]{1,0:T(8,128)(2,1)S(1)} %bitcast.16, bf16[1280,8192]{1,0:T(8,128)(2,1)} %grad.1), custom_call_target="tpu_custom_call" | custom-call | flops 21474836480 | bytes 23592960 | tf_op jit(solution)/shard_map/pallas_call | solution.py:486
  119.5 1.3 %reduce_max.9 = f32[]{:T(128)} reduce(f32[8,128]{1,0:T(8,128)} %get-tuple-element.17, f32[]{:T(128)} %constant.0.clone.1), dimensions={0,1}, to_apply=%region_0.0 | reduce | flops 1023 | bytes 4104 | tf_op jit(solution)/shard_map/reduce_max | solution.py:555
  121.4 0.7 copy.14
  (1 shorter events, 0.0 us)

commit v3 on v2

--- a/solution.py
+++ b/solution.py
@@ -16,7 +16,10 @@
 SEC_A, SEC_B = NX * NY * ROWS_A, NX * NY * ROWS_B
 HALF = SEC_A + SEC_B
 COLS = 256
+SPAN = 512
+WORDS = SPAN // 2
 SLOTS = 8
+PACKED_LAG = (0, 1, 2, 4, 5, 7)
 LAG = (1, 3, 5, 7, 9)
 MESH = pl.DeviceIdType.MESH
 F32, BF16 = jnp.float32, jnp.bfloat16
@@ -240,6 +243,7 @@
 
     sibling = {"local": loc + 1 - 2 * c}
     across = {"local": loc + NC * (1 - 2 * x)}
+    near = [sibling, across, {"local": loc + 1 - 2 * c + NC * (1 - 2 * x)}]
     ring = [at_y((y + k) % NY) for k in (1, 3, 2)]
 
     def remote(src, dst, s, r, device):
@@ -248,7 +252,7 @@
         )
 
     def load(t):
-        cols = pl.ds(pl.multiple_of(t * COLS, COLS), COLS)
+        cols = pl.ds(pl.multiple_of(t * SPAN, SPAN), SPAN)
         return pltpu.make_async_copy(grad.at[:, cols], gbuf.at[t % 3], gsem.at[t % 3])
 
     def core_copy(t):
@@ -279,23 +283,20 @@
             at_y(turn(t, part)[1 - late]),
         )
 
-    def node_send(t, k):
-        to = (me + k) % N_NODE
-        return remote(
-            ns.at[t % SLOTS, to], nr.at[t, me], node_s.at[t % SLOTS, k], node_r.at[t % SLOTS, k], {"node": to}
-        )
-
-    def node_recv(t, k):
-        source = (me + N_NODE - k) % N_NODE
-        return remote(
-            ns.at[t % SLOTS, source], nr.at[t, source],
-            node_s.at[t % SLOTS, k], node_r.at[t % SLOTS, k], {"node": source},
-        )
+    def node_send(group, j):
+        to = (me + j) % N_NODE
+        k = group % SLOTS
+        return remote(ns.at[k, to], nr.at[group, me], node_s.at[k], node_r.at[k], {"node": to})
+
+    def node_all(group):
+        k, count = group % SLOTS, pl.ds(0, N_NODE - 1)
+        return remote(ns.at[k, count], nr.at[group, count], node_s.at[k], node_r.at[k], {"node": (me + 1) % N_NODE})
 
     def pack(first, second, scale):
         both = first + second
         excess = jnp.maximum(jnp.abs(both), jnp.abs(second) * 4096.0) - scale
-        flag[...] = jnp.maximum(flag[...], jnp.max(excess.reshape(-1, 8, QB), axis=0))
+        width = scale.shape[-1]
+        flag[:, :width] = jnp.maximum(flag[:, :width], jnp.max(excess.reshape(-1, 8, width), axis=0))
         return both + jnp.where(both < 0.0, -scale, scale)
 
     def join(left, right):
@@ -305,15 +306,31 @@
         return pl.ds(pl.multiple_of(index * count, 8), count)
 
     barrier = pltpu.get_barrier_semaphore()
-    peers = [sibling, across] + ring + [{"node": (me + k) % N_NODE} for k in range(1, N_NODE)]
+    peers = near + ring + [{"node": (me + k) % N_NODE} for k in range(1, N_NODE)]
     load(0).start()
     load(1).start()
     for peer in peers:
         pl.semaphore_signal(barrier, inc=1, device_id=peer, device_id_type=MESH)
-    flag[...] = jnp.full((8, QB), -1.0, F32)
-    pl.semaphore_wait(barrier, len(peers))
-
-    def compute(t):
+    flag[...] = jnp.full((8, WORDS), -1.0, F32)
+
+    def compute(t, mine):
+        for first in range(0, HALF, 256):
+            start = (c if mine else 1 - c) * HALF + first
+            rows = pl.ds(pl.multiple_of(start, 256), 256)
+            part = jnp.dot(ht[rows, :], gbuf[t % 3], preferred_element_type=F32)
+            for j in range(WORDS // QB):
+                one, unit_one = quantize(part[:, 2 * j * QB : (2 * j + 1) * QB])
+                two, unit_two = quantize(part[:, (2 * j + 1) * QB : (2 * j + 2) * QB])
+                scale = jnp.broadcast_to(jnp.minimum(unit_one, unit_two) * 2.0**23, (256, QB))
+                one = one * 4096.0
+                at = slice(first, first + 256), slice(j * QB, (j + 1) * QB)
+                if mine:
+                    for i, value in enumerate((one, two, scale)):
+                        own[t % 2, i, *at] = value
+                else:
+                    qsend[t % 4, *at] = pack(one, two, scale)
+
+    def compute_theirs(t):
         @pl.when(t + 2 < chunks)
         def _():
             load(t + 2).start()
@@ -324,24 +341,16 @@
         def _():
             core_copy(t - 4).wait_send()
 
-        block = gbuf.at[t % 3]
-        for mine in (0, 1):
-            for first, count in ((0, 256), (256, 256)):
-                start = (c if mine else 1 - c) * HALF + first
-                rows = pl.ds(pl.multiple_of(start, 256), count)
-                part = jnp.dot(ht[rows, :], block[...], preferred_element_type=F32)
-                one, unit_one = quantize(part[:, :QB])
-                two, unit_two = quantize(part[:, QB:])
-                scale = jnp.minimum(unit_one, unit_two) * 2.0**23
-                one = one * 4096.0
-                if mine:
-                    own[t % 2, 0, first : first + count] = one
-                    own[t % 2, 1, first : first + count] = two
-                    own[t % 2, 2, first : first + count] = jnp.broadcast_to(scale, (count, QB))
-                else:
-                    qsend[t % 4, first : first + count] = pack(one, two, scale)
-            if not mine:
-                core_copy(t).start()
+        compute(t, False)
+
+        @pl.when(t == 0)
+        def _():
+            pl.semaphore_wait(barrier, len(peers))
+
+        core_copy(t).start()
+
+    def compute_mine(t):
+        compute(t, True)
 
     def stage1(t):
         k = t % SLOTS
@@ -413,27 +422,38 @@
         xb_copy(t).wait()
         last = unpack(xb[t])
         sum_b = [sb[k, 0, i, :ROWS_B] + last[i] for i in range(2)]
+        group = (t // 2) % SLOTS
         for total, node, count in ((sum_a, 0, NODE_A), (sum_b, NODE_A, NODE_B)):
-            pieces = [
-                quantize(total[0] * (1.0 / 4096.0))[0].reshape(count, 8, QB),
-                quantize(total[1])[0].reshape(count, 8, QB),
-            ]
-            ns[k, node : node + count] = jnp.concatenate(pieces, axis=1).astype(BF16)
-        for j in range(1, N_NODE):
-            node_send(t, j).start()
+            for j in range(WORDS // QB):
+                cut = slice(j * QB, (j + 1) * QB)
+                pieces = [
+                    quantize(total[0][:, cut] * (1.0 / 4096.0))[0].reshape(count, 8, QB),
+                    quantize(total[1][:, cut])[0].reshape(count, 8, QB),
+                ]
+                ns[group, node : node + count, t % 2, :, cut] = jnp.concatenate(pieces, axis=1).astype(BF16)
+
+        @pl.when(t % 2 == 1)
+        def _():
+            for j in range(1, N_NODE):
+                node_send(t // 2, j).start()
 
     def stage5(t):
-        total = ns[t % SLOTS, me].astype(F32)
-        for j in range(1, N_NODE):
-            node_send(t, j).wait_send()
-            node_recv(t, j).wait_recv()
-            total = total + nr[t, (me + N_NODE - j) % N_NODE].astype(F32)
-        for j in range(COLS // QB):
-            cols = pl.ds(pl.multiple_of(t * COLS + j * QB, QB), QB)
-            out[:, cols] = total[8 * j : 8 * j + 8]
-
-    rounds = ([sibling], [across], ring, [{"node": (me + k) % N_NODE} for k in range(1, N_NODE)])
-    places = (0, 1, 2, 5)
+        @pl.when(t % 2 == 1)
+        def _():
+            group = t // 2
+            node_all(group).wait()
+            for part in range(2):
+                total = ns[group % SLOTS, me, part].astype(F32)
+                for j in range(1, N_NODE):
+                    total = total + nr[group, (me + j) % N_NODE, part].astype(F32)
+                for j in range(SPAN // QB):
+                    start = (2 * group + part) * SPAN + j * QB
+                    cols = pl.ds(pl.multiple_of(start, QB), QB)
+                    row, lane = 8 * (j % 2), j // 2 * QB
+                    out[:, cols] = total[row : row + 8, lane : lane + QB]
+
+    rounds = (near, ring, [{"node": (me + k) % N_NODE} for k in range(1, N_NODE)])
+    places = (0, 3, 6)
 
     def flag_copies(index):
         return [
@@ -445,27 +465,36 @@
         ]
 
     def flag_round(index):
-        value = flag[...] if index == 0 else fsend[index - 1]
-        if index:
+        if index == 0:
+            value = functools.reduce(jnp.maximum, [flag[:, j * QB : (j + 1) * QB] for j in range(WORDS // QB)])
+        else:
+            value = fsend[index - 1]
             for i, copy in enumerate(flag_copies(index - 1)):
                 copy.wait()
                 value = jnp.maximum(value, frecv[places[index - 1] + i])
         if index == len(rounds):
-            flag_out[...] = value
+            flag_out[0, 0] = jnp.max(value)
             return
         fsend[index] = value
         for copy in flag_copies(index):
             copy.start()
 
     def step(t, carry):
-        pl.when(t < chunks)(lambda: compute(t))
-        for lag, stage in zip(LAG, (stage1, stage2, stage3, stage4, stage5)):
-            pl.when((t >= lag) & (t < chunks + lag))(functools.partial(stage, t - lag))
+        def run(body, lag):
+            pl.when((t >= lag) & (t < chunks + lag))(lambda: body(t - lag))
+
+        run(compute_theirs, 0)
+        run(stage1, PACKED_LAG[1])
+        run(stage3, PACKED_LAG[3])
         for index in range(len(rounds)):
-            pl.when(t == chunks + LAG[2] + index)(functools.partial(flag_round, index))
+            pl.when(t == chunks - 1 + PACKED_LAG[3] + index)(functools.partial(flag_round, index))
+        run(compute_mine, 0)
+        run(stage2, PACKED_LAG[2])
+        run(stage4, PACKED_LAG[4])
+        run(stage5, PACKED_LAG[5])
         return carry
 
-    lax.fori_loop(0, chunks + LAG[-1], step, 0)
+    lax.fori_loop(0, chunks + PACKED_LAG[-1], step, 0)
     flag_round(len(rounds))
     for t in range(chunks - 4, chunks):
         core_copy(t).wait_send()
@@ -479,15 +508,18 @@
     return jnp.concatenate([first, second], axis=1).reshape(NC * HALF, tokens)
 
 
-def call(body, collective_id, ht, grad_out, extra_out, scratch):
+def call(body, chunks, collective_id, ht, grad_out, has_flag, scratch):
     tokens, width = grad_out.shape
     vmem_spec = pl.BlockSpec(memory_space=pltpu.VMEM)
-    out_shape = [jax.ShapeDtypeStruct((8, width), F32)] + extra_out
+    out_shape, out_specs = [jax.ShapeDtypeStruct((8, width), F32)], [vmem_spec]
+    if has_flag:
+        out_shape.append(jax.ShapeDtypeStruct((1, 1), F32))
+        out_specs.append(pl.BlockSpec(memory_space=pltpu.SMEM))
     return pl.pallas_call(
-        functools.partial(body, width // COLS),
+        functools.partial(body, chunks),
         out_shape=out_shape,
         in_specs=[vmem_spec, pl.BlockSpec(memory_space=pl.ANY)],
-        out_specs=[vmem_spec] * len(out_shape),
+        out_specs=out_specs,
         scratch_shapes=scratch,
         compiler_params=pltpu.CompilerParams(
             collective_id=collective_id, has_side_effects=True, vmem_limit_bytes=58 * 2**20
@@ -522,37 +554,37 @@
         *[dma((SLOTS, 2, 2))] * 4,
         *[dma((SLOTS, N_NODE))] * 2,
     ]
-    return call(wide_kernel, 1, ht, grad_out, [], scratch)[0]
+    return call(wide_kernel, chunks, 1, ht, grad_out, False, scratch)[0]
 
 
 def packed(ht, grad_out):
     tokens, width = grad_out.shape
-    chunks = width // COLS
+    chunks = width // SPAN
     vmem, dma = pltpu.VMEM, pltpu.SemaphoreType.DMA
     sizes = [(NY * ROWS_A,), (ROWS_A,), (2, ROWS_A), (NX * ROWS_B,), (2, NX * ROWS_B), (ROWS_B,)]
     scratch = [
-        vmem((3, tokens, COLS), BF16),
-        vmem((4, HALF, QB), F32),
-        vmem((chunks, HALF, QB), F32),
-        vmem((2, 3, HALF, QB), F32),
-        vmem((SLOTS, 3, NY * ROWS_A, QB), F32),
-        vmem((SLOTS, 2, 3, NX * ROWS_B, QB), F32),
-        *[vmem((SLOTS, *size, QB), F32) for size in sizes],
-        *[vmem((chunks, *size, QB), F32) for size in sizes],
-        vmem((SLOTS, N_NODE, 16, QB), BF16),
-        vmem((chunks, N_NODE, 16, QB), BF16),
-        vmem((8, QB), F32),
-        vmem((4, 8, QB), F32),
-        vmem((12, 8, QB), F32),
+        vmem((3, tokens, SPAN), BF16),
+        vmem((4, HALF, WORDS), F32),
+        vmem((chunks, HALF, WORDS), F32),
+        vmem((2, 3, HALF, WORDS), F32),
+        vmem((SLOTS, 3, NY * ROWS_A, WORDS), F32),
+        vmem((SLOTS, 2, 3, NX * ROWS_B, WORDS), F32),
+        *[vmem((SLOTS, *size, WORDS), F32) for size in sizes],
+        *[vmem((chunks, *size, WORDS), F32) for size in sizes],
+        vmem((SLOTS, N_NODE, 2, 16, WORDS), BF16),
+        vmem((chunks // 2, N_NODE, 2, 16, WORDS), BF16),
+        vmem((8, WORDS), F32),
+        vmem((3, 8, QB), F32),
+        vmem((13, 8, QB), F32),
         dma((3,)),
         *[dma((SLOTS,))] * 2,
         *[dma((SLOTS, 2))] * 4,
         *[dma((SLOTS, 2, 2))] * 2,
-        *[dma((SLOTS, N_NODE))] * 2,
-        *[dma((12,))] * 2,
+        *[dma((SLOTS,))] * 2,
+        *[dma((13,))] * 2,
     ]
-    out, flag = call(packed_kernel, 0, ht, grad_out, [jax.ShapeDtypeStruct((8, QB), F32)], scratch)
-    return out, jnp.max(flag) >= 0.0
+    out, flag = call(packed_kernel, chunks, 0, ht, grad_out, True, scratch)
+    return out, flag[0, 0] >= 0.0
 
 
 def per_device(hidden_acts, grad_out):

time: 122 us -> 91.3 us (0.75)
  Pallas kernels: 116 us -> 86.3 us
  other arithmetic: 1.45 us -> 0.17 us
    pallas_call x1, Pallas kernels: 116 us -> 86.3 us  [call(): pl.pallas_call(functools.partial(body, chunks), out_shape=out_shape, in_s...]
    reduce_max x1 -> x0, other arithmetic: 1.28 us -> none  [packed(): return (out, jnp.max(flag) >= 0.0)]
where the time goes in v3:
time: 91.3 us; the launch traced here: 91.2 us
  Pallas kernels  86.3 us (95%)
  local copies, waits for them, and re-layouts  4.03 us (4%)
    pallas_call x1, Pallas kernels, call(): pl.pallas_call(functools.partial(body, chunks), out_shape=out_shape, in_s...  86.3 us
    unnamed x2, local copies, waits for them, and re-layouts  3.68 us

profile of v3, /device:TPU:0, one launch (start us, length us, event | category | flops | bytes accessed | tf_op | source)
XLA Modules:
  0.0 91.2 jit_solution(15692969288143676610)
XLA Ops:
  0.0 3.0 %copy.8 = bf16[1280,1024]{0,1:T(8,128)(2,1)S(1)} copy(bf16[1280,1024]{1,0:T(8,128)(2,1)} %param.4) | data formatting | bytes 5242880 | tf_op args[0]
  3.0 0.1 slice.16
  3.1 0.1 slice.17
  3.2 0.1 copy.10
  3.3 0.1 copy.9
  3.4 0.2 pad_maximum_fusion
  3.5 86.3 %shard_map.30 = (f32[8,8192]{1,0:T(8,128)S(1)}, f32[1,1]{1,0:T(1,128)}) custom-call(bf16[1024,1280]{1,0:T(8,128)(2,1)S(1)} %bitcast.17, bf16[1280,8192]{1,0:T(8,128)(2,1)} %grad.1), custom_call_target="tpu_custom_call" | custom-call | flops 21474836480 | bytes 23592960 | tf_op jit(solution)/shard_map/pallas_call | solution.py:518
  90.4 0.7 copy.14
  (1 shorter events, 0.0 us)

commit v4 on v3

--- a/solution.py
+++ b/solution.py
@@ -19,21 +19,24 @@
 SPAN = 512
 WORDS = SPAN // 2
 SLOTS = 8
-PACKED_LAG = (0, 1, 2, 4, 5, 7)
+PACKED_LAG = (0, 1, 2, 4, 5, 7, 8)
+NZ, NX_HI = 4, 2
 LAG = (1, 3, 5, 7, 9)
 MESH = pl.DeviceIdType.MESH
 F32, BF16 = jnp.float32, jnp.bfloat16
 
 
-def quantize(values):
+def block_levels(values):
     peak = jnp.max(jnp.abs(values), axis=-1, keepdims=True)
     scaled = peak * (2.0**23 + 1.0)
-    power = scaled - scaled * (1.0 - 2.0**-24)
-    power = jnp.minimum(jnp.maximum(power, 2.0**-64), 2.0**63)
+    power = jnp.maximum(scaled - scaled * (1.0 - 2.0**-24), 2.0**-64)
     levels = jnp.floor(values * (64.0 / power) + 0.5)
-    unit = power * (1.0 / 64.0)
-    levels = jnp.minimum(jnp.maximum(levels, -127.0), 127.0)
-    return levels * unit, jnp.where(peak > 0.0, unit, 2.0**57)
+    return jnp.minimum(jnp.maximum(levels, -127.0), 127.0), power
+
+
+def quantize(values):
+    levels, power = block_levels(values)
+    return levels * (power * (1.0 / 64.0))
 
 
 def wide_kernel(
@@ -141,7 +144,7 @@
             part = jnp.dot(ht[rows, :], block[...], preferred_element_type=F32)
             for j in range(COLS // QB):
                 cut = slice(j * QB, (j + 1) * QB)
-                qsend[t % 4, first : first + count, cut] = quantize(part[:, cut])[0].astype(BF16)
+                qsend[t % 4, first : first + count, cut] = quantize(part[:, cut]).astype(BF16)
         core_copy(t).start()
         for first, count, dst, shape in (
             (0, SEC_A, sa, (NX, NY, ROWS_A, QB)),
@@ -151,7 +154,7 @@
             part = jnp.dot(ht[rows, :], block[...], preferred_element_type=F32)
             for j in range(COLS // QB):
                 cut = slice(j * QB, (j + 1) * QB)
-                dst[t, :, :, :, cut] = quantize(part[:, cut])[0].reshape(shape)
+                dst[t, :, :, :, cut] = quantize(part[:, cut]).reshape(shape)
 
     def stage1(t):
         core_copy(t).wait_recv()
@@ -185,7 +188,7 @@
         sum_b = sb[t, y, x] + xb[t]
         for total, node, count in ((sum_a, 0, NODE_A), (sum_b, NODE_A, NODE_B)):
             pieces = [
-                quantize(total[:, j * QB : (j + 1) * QB])[0].reshape(count, 8, QB) for j in range(COLS // QB)
+                quantize(total[:, j * QB : (j + 1) * QB]).reshape(count, 8, QB) for j in range(COLS // QB)
             ]
             ns[t, node : node + count] = jnp.concatenate(pieces, axis=1).astype(BF16)
         for k in range(1, N_NODE):
@@ -229,22 +232,29 @@
 def packed_kernel(
     chunks, ht, grad, out, flag_out,
     gbuf, qsend, qrecv, own, sa, sb,
-    xas, y1as, y2as, y1bs, y2bs, xbs, xa, y1a, y2a, y1b, y2b, xb, ns, nr, flag, fsend, frecv,
-    gsem, core_s, core_r, x_s, x_r, y1_s, y1_r, y2_s, y2_r, node_s, node_r, flag_s, flag_r,
+    xas, y1as, y2as, y1bs, y2bs, xbs, xa, y1a, y2a, y1b, y2b, xb, ns, nr, held, hs, hr, direct, flag, fsend, frecv,
+    gsem, core_s, core_r, x_s, x_r, y1_s, y1_r, y2_s, y2_r, node_s, node_r, half_s, half_r, direct_s, direct_r, flag_s, flag_r,
 ):
     me = lax.axis_index("node")
     loc = lax.axis_index("local")
-    c, x, y = loc % NC, (loc // NC) % NX, loc // (NC * NX)
-    far = (y + 2) % NY
+    c, x, y = lax.rem(loc, NC), lax.rem(lax.div(loc, NC), NX), lax.div(loc, NC * NX)
+    far, sides = lax.rem(y + 2, NY), (lax.rem(y + 1, NY), lax.rem(y + 3, NY))
     other = 1 - x
+    x_hi, z = lax.div(me, NZ), lax.rem(me, NZ)
+    relayed = chunks // 4
+    opposite = {"node": me + NZ * (1 - 2 * x_hi)}
 
     def at_y(row):
         return {"local": (row * NX + x) * NC + c}
 
     sibling = {"local": loc + 1 - 2 * c}
     across = {"local": loc + NC * (1 - 2 * x)}
-    near = [sibling, across, {"local": loc + 1 - 2 * c + NC * (1 - 2 * x)}]
-    ring = [at_y((y + k) % NY) for k in (1, 3, 2)]
+    ring = [at_y(row) for row in sides]
+    mates = [
+        {"local": (lax.rem(y + j // 4, NY) * NX + lax.rem(x + j // 2 % 2, NX)) * NC + lax.rem(c + j % 2, NC)}
+        for j in range(1, NY * NX * NC)
+    ]
+    nodes = [{"node": lax.rem(x_hi + j // NZ, NX_HI) * NZ + lax.rem(z + j % NZ, NZ)} for j in range(1, N_NODE)]
 
     def remote(src, dst, s, r, device):
         return pltpu.make_async_remote_copy(
@@ -253,44 +263,11 @@
 
     def load(t):
         cols = pl.ds(pl.multiple_of(t * SPAN, SPAN), SPAN)
-        return pltpu.make_async_copy(grad.at[:, cols], gbuf.at[t % 3], gsem.at[t % 3])
-
-    def core_copy(t):
-        return remote(qsend.at[t % 4], qrecv.at[t], core_s.at[t % SLOTS], core_r.at[t % SLOTS], sibling)
-
-    def turn(t, part):
-        odd = (t + part) % 2
-        return (y + 1 + 2 * odd) % NY, (y + 3 - 2 * odd) % NY
-
-    def xa_copy(t):
-        k = t % SLOTS
-        return remote(xas.at[k], xa.at[t], x_s.at[k, 0], x_r.at[k, 0], across)
-
-    def xb_copy(t):
-        k = t % SLOTS
-        return remote(xbs.at[k], xb.at[t], x_s.at[k, 1], x_r.at[k, 1], across)
-
-    def y1_copy(t, part):
-        k = t % SLOTS
-        src, dst = ((y1as, y1a), (y1bs, y1b))[part]
-        return remote(src.at[k], dst.at[t], y1_s.at[k, part], y1_r.at[k, part], at_y(turn(t, part)[0]))
-
-    def y2_copy(t, part, late):
-        k = t % SLOTS
-        src, dst = ((y2as, y2a), (y2bs, y2b))[part]
-        return remote(
-            src.at[k, late], dst.at[t, late], y2_s.at[k, part, late], y2_r.at[k, part, late],
-            at_y(turn(t, part)[1 - late]),
-        )
-
-    def node_send(group, j):
-        to = (me + j) % N_NODE
-        k = group % SLOTS
-        return remote(ns.at[k, to], nr.at[group, me], node_s.at[k], node_r.at[k], {"node": to})
-
-    def node_all(group):
-        k, count = group % SLOTS, pl.ds(0, N_NODE - 1)
-        return remote(ns.at[k, count], nr.at[group, count], node_s.at[k], node_r.at[k], {"node": (me + 1) % N_NODE})
+        return pltpu.make_async_copy(grad.at[:, cols], gbuf.at[lax.rem(t, 3)], gsem.at[lax.rem(t, 3)])
+
+    def turn(t):
+        odd = lax.rem(t, 2)
+        return lax.rem(y + 1 + 2 * odd, NY), lax.rem(y + 3 - 2 * odd, NY)
 
     def pack(first, second, scale):
         both = first + second
@@ -306,41 +283,101 @@
         return pl.ds(pl.multiple_of(index * count, 8), count)
 
     barrier = pltpu.get_barrier_semaphore()
-    peers = near + ring + [{"node": (me + k) % N_NODE} for k in range(1, N_NODE)]
+    peers = mates + nodes
     load(0).start()
     load(1).start()
     for peer in peers:
         pl.semaphore_signal(barrier, inc=1, device_id=peer, device_id_type=MESH)
     flag[...] = jnp.full((8, WORDS), -1.0, F32)
 
+    def core_copy(t):
+        k = lax.rem(t, SLOTS)
+        return remote(qsend.at[lax.rem(t, 2)], qrecv.at[t], core_s.at[k], core_r.at[k], sibling)
+
+    def xa_copy(t):
+        k = lax.rem(t, SLOTS)
+        return remote(xas.at[k], xa.at[t], x_s.at[k, 0], x_r.at[k, 0], across)
+
+    def xb_copy(t):
+        k = lax.rem(t, SLOTS)
+        return remote(xbs.at[k], xb.at[t], x_s.at[k, 1], x_r.at[k, 1], across)
+
+    def y1a_copy(t):
+        k = lax.rem(t, SLOTS)
+        return remote(y1as.at[k], y1a.at[t], y1_s.at[k, 2], y1_r.at[k, 2], at_y(turn(t)[0]))
+
+    def y1b_copy(t, d):
+        k = lax.rem(t, SLOTS)
+        return remote(y1bs.at[k, d], y1b.at[t, d], y1_s.at[k, d], y1_r.at[k, d], ring[d])
+
+    def y2a_copy(t, late):
+        k = lax.rem(t, SLOTS)
+        return remote(
+            y2as.at[k, late], y2a.at[t, late], y2_s.at[k, 2, late], y2_r.at[k, 2, late], at_y(turn(t)[1 - late])
+        )
+
+    def y2b_copy(t, d, late):
+        k = lax.rem(t, SLOTS)
+        return remote(
+            y2bs.at[k, d, late], y2b.at[t, d, late], y2_s.at[k, d, late], y2_r.at[k, d, late], ring[d]
+        )
+
+    def z_copies(group):
+        k = lax.rem(group, SLOTS)
+        return [
+            remote(
+                ns.at[k, lax.rem(z + j, NZ)], nr.at[group, z],
+                node_s.at[k], node_r.at[k], {"node": x_hi * NZ + lax.rem(z + j, NZ)},
+            )
+            for j in range(1, NZ)
+        ]
+
+    def z_all(group):
+        k, count = lax.rem(group, SLOTS), pl.ds(0, NZ - 1)
+        return remote(
+            ns.at[k, count], nr.at[group, count],
+            node_s.at[k], node_r.at[k], opposite,
+        )
+
+    def direct_copies(group):
+        k, g = lax.rem(group, SLOTS), group - relayed
+        return [
+            remote(
+                ns.at[k, lax.rem(z + j % NZ, NZ), lax.rem(x_hi + j // NZ, NX_HI)], direct.at[g, j],
+                direct_s.at[g], direct_r.at[g],
+                {"node": lax.rem(x_hi + j // NZ, NX_HI) * NZ + lax.rem(z + j % NZ, NZ)},
+            )
+            for j in range(1, N_NODE)
+        ]
+
+    def half_copy(group):
+        k = lax.rem(group, SLOTS)
+        return remote(hs.at[k], hr.at[group], half_s.at[k], half_r.at[k], opposite)
+
     def compute(t, mine):
-        for first in range(0, HALF, 256):
+        for first in range(0, HALF, 128):
             start = (c if mine else 1 - c) * HALF + first
-            rows = pl.ds(pl.multiple_of(start, 256), 256)
-            part = jnp.dot(ht[rows, :], gbuf[t % 3], preferred_element_type=F32)
+            rows = pl.ds(pl.multiple_of(start, 128), 128)
+            part = jnp.dot(ht[rows, :], gbuf[lax.rem(t, 3)], preferred_element_type=F32)
             for j in range(WORDS // QB):
-                one, unit_one = quantize(part[:, 2 * j * QB : (2 * j + 1) * QB])
-                two, unit_two = quantize(part[:, (2 * j + 1) * QB : (2 * j + 2) * QB])
-                scale = jnp.broadcast_to(jnp.minimum(unit_one, unit_two) * 2.0**23, (256, QB))
-                one = one * 4096.0
-                at = slice(first, first + 256), slice(j * QB, (j + 1) * QB)
+                one, power_one = block_levels(part[:, 2 * j * QB : (2 * j + 1) * QB])
+                two, power_two = block_levels(part[:, (2 * j + 1) * QB : (2 * j + 2) * QB])
+                one, two = one * (power_one * 64.0), two * (power_two * (1.0 / 64.0))
+                least = jnp.minimum(power_one, power_two)
+                scale = jnp.broadcast_to(least * 2.0**17, (128, QB))
+                at = slice(first, first + 128), slice(j * QB, (j + 1) * QB)
                 if mine:
                     for i, value in enumerate((one, two, scale)):
-                        own[t % 2, i, *at] = value
+                        own[lax.rem(t, 2), i, *at] = value
                 else:
-                    qsend[t % 4, *at] = pack(one, two, scale)
+                    excess = jnp.maximum(power_one, power_two) - least * 32.0
+                    flag[:, :QB] = jnp.maximum(flag[:, :QB], jnp.max(excess.reshape(-1, 8, 1), axis=0))
+                    both = one + two
+                    qsend[lax.rem(t, 2), *at] = both + jnp.where(both < 0.0, -scale, scale)
 
     def compute_theirs(t):
-        @pl.when(t + 2 < chunks)
-        def _():
-            load(t + 2).start()
-
+        pl.when(t + 2 < chunks)(lambda: load(t + 2).start())
         load(t).wait()
-
-        @pl.when(t >= 4)
-        def _():
-            core_copy(t - 4).wait_send()
-
         compute(t, False)
 
         @pl.when(t == 0)
@@ -353,107 +390,138 @@
         compute(t, True)
 
     def stage1(t):
-        k = t % SLOTS
-        core_copy(t).wait_recv()
+        k = lax.rem(t, SLOTS)
+        core_copy(t).wait()
 
         def pair(first, index, count):
             rows = pl.ds(pl.multiple_of(first + index * count, 8), count)
-            return join(unpack(qrecv[t, rows]), tuple(own[t % 2, i, rows] for i in range(3)))
-
+            return join(unpack(qrecv[t, rows]), tuple(own[lax.rem(t, 2), i, rows] for i in range(3)))
+
+        for d in range(2):
+            y1bs[k, d] = pack(*pair(SEC_A, far * NX + d, ROWS_B))
+            y1b_copy(t, d).start()
         xas[k] = pack(*pair(0, other, NY * ROWS_A))
         xa_copy(t).start()
-        ahead, behind = turn(t, 1)
-        y1bs[k] = pack(*pair(SEC_A, far, NX * ROWS_B))
-        y1_copy(t, 1).start()
-        y2bs[k, 0] = pack(*pair(SEC_A, behind, NX * ROWS_B))
-        y2_copy(t, 1, 0).start()
+        for d in range(2):
+            y2bs[k, d, 0] = pack(*pair(SEC_A, sides[d] * NX + 1 - d, ROWS_B))
+            y2b_copy(t, d, 0).start()
         for i, value in enumerate(pair(0, x, NY * ROWS_A)):
             sa[k, i] = value
-        for j, row in enumerate((ahead, y)):
-            for i, value in enumerate(pair(SEC_A, row, NX * ROWS_B)):
+        for j, index in enumerate((sides[0] * NX, sides[1] * NX + 1, y * NX, y * NX + 1)):
+            for i, value in enumerate(pair(SEC_A, index, ROWS_B)):
                 sb[k, j, i] = value
 
     def stage2(t):
-        k = t % SLOTS
+        k = lax.rem(t, SLOTS)
+        for d in range(2):
+            y1b_copy(t, d).wait()
+            y2bs[k, d, 1] = pack(*join(unpack(y1b[t, d]), tuple(sb[k, d, i] for i in range(3))))
+            y2b_copy(t, d, 1).start()
         xa_copy(t).wait()
 
         def pair(row):
             rows = rows_of(row, ROWS_A)
             return join(unpack(xa[t, rows]), tuple(sa[k, i, rows] for i in range(3)))
 
-        ahead, behind = turn(t, 0)
+        ahead, behind = turn(t)
         y1as[k] = pack(*pair(far))
-        y1_copy(t, 0).start()
+        y1a_copy(t).start()
         y2as[k, 0] = pack(*pair(behind))
-        y2_copy(t, 0, 0).start()
+        y2a_copy(t, 0).start()
         for row in (ahead, y):
             for i, value in enumerate(pair(row)):
                 sa[k, i, rows_of(row, ROWS_A)] = value
-        y1_copy(t, 1).wait()
-        y2bs[k, 1] = pack(*join(unpack(y1b[t]), tuple(sb[k, 0, i] for i in range(3))))
-        y2_copy(t, 1, 1).start()
 
     def stage3(t):
-        k = t % SLOTS
-        y1_copy(t, 0).wait()
-        rows = rows_of(turn(t, 0)[0], ROWS_A)
+        k = lax.rem(t, SLOTS)
+        y1a_copy(t).wait()
+        rows = rows_of(turn(t)[0], ROWS_A)
         y2as[k, 1] = pack(*join(unpack(y1a[t]), tuple(sa[k, i, rows] for i in range(3))))
-        y2_copy(t, 0, 1).start()
-        y2_copy(t, 1, 0).wait()
-        y2_copy(t, 1, 1).wait()
+        y2a_copy(t, 1).start()
+        for d in range(2):
+            for late in range(2):
+                y2b_copy(t, d, late).wait()
 
         def pair(index):
-            rows = rows_of(index, ROWS_B)
-            held = tuple(sb[k, 1, i, rows] for i in range(3))
-            return join(join(unpack(y2b[t, 0, rows]), unpack(y2b[t, 1, rows])), held)
+            mine = tuple(sb[k, 2 + index, i] for i in range(3))
+            return join(join(unpack(y2b[t, 0, 1 - index]), unpack(y2b[t, 1, index])), mine)
 
         xbs[k] = pack(*pair(other))
         xb_copy(t).start()
         for i, value in enumerate(pair(x)[:2]):
-            sb[k, 0, i, :ROWS_B] = value
+            sb[k, 0, i] = value
 
     def stage4(t):
-        k = t % SLOTS
-        y2_copy(t, 0, 0).wait()
-        y2_copy(t, 0, 1).wait()
+        k = lax.rem(t, SLOTS)
+        y2a_copy(t, 0).wait()
+        y2a_copy(t, 1).wait()
         rows = rows_of(y, ROWS_A)
         left, right = unpack(y2a[t, 0]), unpack(y2a[t, 1])
         sum_a = [sa[k, i, rows] + left[i] + right[i] for i in range(2)]
         xb_copy(t).wait()
         last = unpack(xb[t])
-        sum_b = [sb[k, 0, i, :ROWS_B] + last[i] for i in range(2)]
-        group = (t // 2) % SLOTS
-        for total, node, count in ((sum_a, 0, NODE_A), (sum_b, NODE_A, NODE_B)):
-            for j in range(WORDS // QB):
-                cut = slice(j * QB, (j + 1) * QB)
+        sum_b = [sb[k, 0, i] + last[i] for i in range(2)]
+        group = lax.rem(lax.div(t, 2), SLOTS)
+        for j in range(WORDS // QB):
+            cut = slice(j * QB, (j + 1) * QB)
+            for total, node, count in ((sum_a, 0, NODE_A), (sum_b, NODE_A, NODE_B)):
                 pieces = [
-                    quantize(total[0][:, cut] * (1.0 / 4096.0))[0].reshape(count, 8, QB),
-                    quantize(total[1][:, cut])[0].reshape(count, 8, QB),
+                    quantize(total[0][:, cut] * (1.0 / 4096.0)).reshape(count, 8, QB),
+                    quantize(total[1][:, cut]).reshape(count, 8, QB),
                 ]
-                ns[group, node : node + count, t % 2, :, cut] = jnp.concatenate(pieces, axis=1).astype(BF16)
-
-        @pl.when(t % 2 == 1)
+                blocks = jnp.concatenate(pieces, axis=1).astype(BF16)
+                for n in range(count):
+                    ns[group, (node + n) % NZ, (node + n) // NZ, lax.rem(t, 2), :, cut] = blocks[n]
+
+        @pl.when((lax.rem(t, 2) == 1) & (t < 2 * relayed))
         def _():
-            for j in range(1, N_NODE):
-                node_send(t // 2, j).start()
+            for copy in z_copies(lax.div(t, 2)):
+                copy.start()
+
+        @pl.when((lax.rem(t, 2) == 1) & (t >= 2 * relayed))
+        def _():
+            for copy in direct_copies(lax.div(t, 2)):
+                copy.start()
 
     def stage5(t):
-        @pl.when(t % 2 == 1)
-        def _():
-            group = t // 2
-            node_all(group).wait()
-            for part in range(2):
-                total = ns[group % SLOTS, me, part].astype(F32)
-                for j in range(1, N_NODE):
-                    total = total + nr[group, (me + j) % N_NODE, part].astype(F32)
-                for j in range(SPAN // QB):
-                    start = (2 * group + part) * SPAN + j * QB
-                    cols = pl.ds(pl.multiple_of(start, QB), QB)
-                    row, lane = 8 * (j % 2), j // 2 * QB
-                    out[:, cols] = total[row : row + 8, lane : lane + QB]
-
-    rounds = (near, ring, [{"node": (me + k) % N_NODE} for k in range(1, N_NODE)])
-    places = (0, 3, 6)
+        group = lax.div(t, 2)
+        k = lax.rem(group, SLOTS)
+        z_all(group).wait()
+
+        def total(index):
+            value = ns[k, z, index, :].astype(F32)
+            for j in range(1, NZ):
+                value = value + nr[group, lax.rem(z + j, NZ), index, :].astype(F32)
+            return value
+
+        hs[k, :] = total(1 - x_hi)
+        half_copy(group).start()
+        held[k, :] = total(x_hi)
+
+    def stage6(t):
+        group = lax.div(t, 2)
+        k = lax.rem(group, SLOTS)
+        half_copy(group).wait()
+        for part in range(2):
+            store(t - 1 + part, held[k, part] + hr[group, part])
+
+    def store(t, total):
+        for j in range(SPAN // QB):
+            cols = pl.ds(pl.multiple_of(t * SPAN + j * QB, QB), QB)
+            row, lane = 8 * (j % 2), j // 2 * QB
+            out[:, cols] = total[row : row + 8, lane : lane + QB]
+
+    def finish(group):
+        g, count = group - relayed, pl.ds(1, N_NODE - 1)
+        remote(direct.at[g, count], direct.at[g, count], direct_s.at[g], direct_r.at[g], opposite).wait()
+        total = ns[group % SLOTS, z, x_hi].astype(F32)
+        for j in range(1, N_NODE):
+            total = total + direct[g, j].astype(F32)
+        for part in range(2):
+            store(2 * group + part, total[part])
+
+    rounds = (mates, nodes)
+    places = (0, len(mates))
 
     def flag_copies(index):
         return [
@@ -480,24 +548,30 @@
             copy.start()
 
     def step(t, carry):
-        def run(body, lag):
-            pl.when((t >= lag) & (t < chunks + lag))(lambda: body(t - lag))
+        def run(body, stage, end=chunks, odd=False):
+            now = t - PACKED_LAG[stage]
+            inside = (now >= 0) & (now < end)
+            if odd:
+                inside = inside & (lax.rem(t, 2) == (PACKED_LAG[stage] + 1) % 2)
+            pl.when(inside)(lambda: body(now))
 
         run(compute_theirs, 0)
-        run(stage1, PACKED_LAG[1])
-        run(stage3, PACKED_LAG[3])
-        for index in range(len(rounds)):
-            pl.when(t == chunks - 1 + PACKED_LAG[3] + index)(functools.partial(flag_round, index))
+        pl.when((t >= 2) & (t <= chunks))(lambda: stage1(t - 1))
+        run(stage3, 3)
+        pl.when(t == chunks - 1 + PACKED_LAG[3])(lambda: flag_round(0))
         run(compute_mine, 0)
-        run(stage2, PACKED_LAG[2])
-        run(stage4, PACKED_LAG[4])
-        run(stage5, PACKED_LAG[5])
+        pl.when(t == 0)(lambda: stage1(t))
+        run(stage2, 2)
+        run(stage4, 4)
+        pl.when(t == chunks - 1 + PACKED_LAG[4])(lambda: flag_round(1))
+        run(stage5, 5, 2 * relayed, True)
+        run(stage6, 6, 2 * relayed, True)
         return carry
 
-    lax.fori_loop(0, chunks + PACKED_LAG[-1], step, 0)
-    flag_round(len(rounds))
-    for t in range(chunks - 4, chunks):
-        core_copy(t).wait_send()
+    lax.fori_loop(0, chunks + PACKED_LAG[4], step, 0)
+    for group in range(relayed, chunks // 2):
+        finish(group)
+    flag_round(2)
 
 
 def arrange(hidden_acts):
@@ -561,27 +635,33 @@
     tokens, width = grad_out.shape
     chunks = width // SPAN
     vmem, dma = pltpu.VMEM, pltpu.SemaphoreType.DMA
-    sizes = [(NY * ROWS_A,), (ROWS_A,), (2, ROWS_A), (NX * ROWS_B,), (2, NX * ROWS_B), (ROWS_B,)]
+    sizes = [(NY * ROWS_A,), (ROWS_A,), (2, ROWS_A), (2, ROWS_B), (2, 2, ROWS_B), (ROWS_B,)]
     scratch = [
         vmem((3, tokens, SPAN), BF16),
-        vmem((4, HALF, WORDS), F32),
+        vmem((2, HALF, WORDS), F32),
         vmem((chunks, HALF, WORDS), F32),
         vmem((2, 3, HALF, WORDS), F32),
         vmem((SLOTS, 3, NY * ROWS_A, WORDS), F32),
-        vmem((SLOTS, 2, 3, NX * ROWS_B, WORDS), F32),
+        vmem((SLOTS, 4, 3, ROWS_B, WORDS), F32),
         *[vmem((SLOTS, *size, WORDS), F32) for size in sizes],
         *[vmem((chunks, *size, WORDS), F32) for size in sizes],
-        vmem((SLOTS, N_NODE, 2, 16, WORDS), BF16),
-        vmem((chunks // 2, N_NODE, 2, 16, WORDS), BF16),
+        vmem((SLOTS, NZ, NX_HI, 2, 16, WORDS), BF16),
+        vmem((chunks // 2, NZ, NX_HI, 2, 16, WORDS), BF16),
+        vmem((SLOTS, 2, 16, WORDS), F32),
+        vmem((SLOTS, 2, 16, WORDS), F32),
+        vmem((chunks // 2, 2, 16, WORDS), F32),
+        vmem((chunks // 2 - chunks // 4, N_NODE, 2, 16, WORDS), BF16),
         vmem((8, WORDS), F32),
-        vmem((3, 8, QB), F32),
-        vmem((13, 8, QB), F32),
+        vmem((2, 8, QB), F32),
+        vmem((22, 8, QB), F32),
         dma((3,)),
         *[dma((SLOTS,))] * 2,
-        *[dma((SLOTS, 2))] * 4,
-        *[dma((SLOTS, 2, 2))] * 2,
-        *[dma((SLOTS,))] * 2,
-        *[dma((13,))] * 2,
+        *[dma((SLOTS, 2))] * 2,
+        *[dma((SLOTS, 3))] * 2,
+        *[dma((SLOTS, 3, 2))] * 2,
+        *[dma((SLOTS,))] * 4,
+        *[dma((chunks // 2 - chunks // 4,))] * 2,
+        *[dma((22,))] * 2,
     ]
     out, flag = call(packed_kernel, chunks, 0, ht, grad_out, True, scratch)
     return out, flag[0, 0] >= 0.0

time: 91.3 us -> 89.4 us (0.979)
  Pallas kernels: 86.3 us -> 84.2 us
    pallas_call x1, Pallas kernels: 86.3 us -> 84.2 us  [call(): pl.pallas_call(functools.partial(body, chunks), out_shape=out_shape, in_s...]
where the time goes in v4:
time: 89.4 us; the launch traced here: 89.1 us
  Pallas kernels  84.2 us (94%)
  local copies, waits for them, and re-layouts  4.03 us (5%)
    pallas_call x1, Pallas kernels, call(): pl.pallas_call(functools.partial(body, chunks), out_shape=out_shape, in_s...  84.2 us
    unnamed x2, local copies, waits for them, and re-layouts  3.68 us

profile of v4, /device:TPU:0, one launch (start us, length us, event | category | flops | bytes accessed | tf_op | source)
XLA Modules:
  0.0 89.1 jit_solution(4216253081791816966)
XLA Ops:
  0.0 3.0 %copy.8 = bf16[1280,1024]{0,1:T(8,128)(2,1)S(1)} copy(bf16[1280,1024]{1,0:T(8,128)(2,1)} %param.4) | data formatting | bytes 5242880 | tf_op args[0]
  3.0 0.1 slice.16
  3.1 0.1 slice.17
  3.2 0.1 copy.10
  3.3 0.1 copy.9
  3.4 0.2 pad_maximum_fusion
  3.5 84.2 %shard_map.30 = (f32[8,8192]{1,0:T(8,128)S(1)}, f32[1,1]{1,0:T(1,128)}) custom-call(bf16[1024,1280]{1,0:T(8,128)(2,1)S(1)} %bitcast.17, bf16[1280,8192]{1,0:T(8,128)(2,1)} %grad.1), custom_call_target="tpu_custom_call" | custom-call | flops 21474836480 | bytes 23592960 | tf_op jit(solution)/shard_map/pallas_call | solution.py:592
  88.4 0.7 copy.14
  (1 shorter events, 0.0 us)
